TPU v7x, 32 devices: a whole 2x2x4 slice. The times are simulated.
32 devices in a mesh: groups: 2 (over y), blk: 4 (over z), panel: 4 (over x, core).
Axes of the slice: x: 2, y: 2, z: 4, core: 2. Of those that a mesh axis runs over, the one named last changes fastest.
Arguments:
- test_features: bfloat16 [2048, 8192], P(('groups', 'blk'), 'panel'), parts along dimension 0, may hold values from -6 to 6
- train_features: bfloat16 [2048, 8192], P(('groups', 'blk'), 'panel'), parts along dimension 0, may hold values from -0.0625 to 0.0625
- kernel_inverse: bfloat16 [8192, 8192], P('panel', 'blk'), as said below
Outputs:
- scores: float32 [2048, 1024], P(('groups', 'panel'), 'blk'), parts along dimension 0
There are 2 independent parts, one for each index of `groups`. A program takes and returns all parts, laid end to end along the dimension named above; an argument that names none is the same for every part. Nothing has to cross between parts.
Inputs may be any that keep to these rules, and one draw needn't show every extreme that they name: kernel_inverse is symmetric.
All inputs are finite; a program needn't handle non-finite values.
Results may differ from a plain program's by a relative error of at most 0.0029.
Values may be sent and summed in bfloat16 or wider, within the bound.
A program may use at most 128 MiB of HBM per device.

v0:
```python
import jax
import jax.numpy as jnp
from jax import lax
from jax.sharding import PartitionSpec as P


def local(test_features, train_features, kernel_inverse):
    all_rows = lax.all_gather(test_features, "blk", axis=0, tiled=True)
    slab_terms = jnp.dot(all_rows, kernel_inverse, preferred_element_type=jnp.float32)
    reduced = lax.psum_scatter(slab_terms, "panel", scatter_dimension=0, tiled=True).astype(
        jnp.bfloat16
    )
    preconditioned = lax.all_to_all(
        lax.all_to_all(reduced, "blk", split_axis=0, concat_axis=1, tiled=True),
        "panel",
        split_axis=1,
        concat_axis=0,
        tiled=True,
    )
    partial_scores = lax.dot_general(
        lax.all_gather(preconditioned, "blk", axis=0, tiled=True),
        train_features,
        (((1,), (1,)), ((), ())),
        preferred_element_type=jnp.float32,
    )
    blocks = lax.axis_size("blk")
    panels = lax.axis_size("panel")
    total_rows = partial_scores.shape[0]
    width = partial_scores.shape[1]
    grouped = partial_scores.reshape(blocks, panels, total_rows // (blocks * panels), width)
    partial_scores = jnp.transpose(grouped, (1, 0, 2, 3)).reshape(total_rows, width)
    return lax.psum_scatter(partial_scores, "panel", scatter_dimension=0, tiled=True)


def solution(mesh):
    in_specs = (P(("groups", "blk"), "panel"), P(("groups", "blk"), "panel"), P("panel", "blk"))
    out_specs = P(("groups", "panel"), "blk")
    return jax.shard_map(local, mesh=mesh, in_specs=in_specs, out_specs=out_specs, check_vma=False)
```

profile of v0, /device:TPU:1, one launch (start us, length us, event | category | flops | bytes accessed | tf_op | source)
XLA Modules:
  0.0 339.8 jit_solution(10063871245489719874)
XLA Ops:
  6.5 0.0 copy-start
  6.5 0.0 all-gather.3.cloned.1.call-start
  6.5 0.7 all-gather.3.cloned.1.call-update
  7.3 0.0 reduce-scatter.3.cloned.1.call-start
  7.3 84.5 %all-gather.3.cloned.1.call-done = bf16[1024,2048]{1,0:T(8,128)(2,1)} async-done(((bf16[256,2048]{1,0:T(8,128)(2,1)}), bf16[1024,2048]{1,0:T(8,128)(2,1)}) %all-gather.3.cloned.1.call-update) | async-done | bytes 4194320 | tf_op jit(solution)/shard_map/all_gather | solution.py:8
  91.8 14.4 %fusion = f32[1024,2048]{1,0:T(8,128)} fusion(bf16[1024,2048]{1,0:T(8,128)(2,1)} %all-gather.3.cloned.1.call-done, bf16[2048,2048]{1,0:T(8,128)(2,1)} %param.5), kind=kOutput, calls=%fused_computation | convolution fusion | flops 8589934592 | bytes 20971520 | tf_op jit(solution)/shard_map/dot_general | solution.py:9
  106.2 0.0 reduce-scatter.3.cloned.1.call-update
  106.3 0.0 all-gather.5.cloned.1.call-start
  106.3 70.3 %reduce-scatter.3.cloned.1.call-done = f32[256,2048]{1,0:T(8,128)} async-done(((f32[1024,2048]{1,0:T(8,128)}), f32[256,2048]{1,0:T(8,128)}) %reduce-scatter.3.cloned.1.call-update) | async-done | bytes 2097168 | tf_op jit(solution)/shard_map/reduce_scatter | solution.py:10
  176.6 1.7 convert_element_type.3
  178.4 29.0 %all_to_all.32 = bf16[4,64,2048]{2,1,0:T(8,128)(2,1)S(1)} all-to-all(bf16[4,64,2048]{2,1,0:T(8,128)(2,1)S(1)} %bitcast.13), channel_id=1, replica_groups=mesh['groups'=2,'blk'=4,'panel'=4] {'blk'}, dimensions={0} | all-to-all | bytes 2097152 | tf_op jit(solution)/shard_map/all_to_all | solution.py:14
  207.3 18.4 %all_to_all.33 = bf16[64,4,2048]{2,0,1:T(8,128)(2,1)} all-to-all(bf16[64,4,2048]{2,0,1:T(8,128)(2,1)S(1)} %bitcast.16), channel_id=1, replica_groups=mesh['groups'=2,'blk'=4,'panel'=4] {'panel'}, dimensions={1} | all-to-all | bytes 2097152 | tf_op jit(solution)/shard_map/all_to_all | solution.py:13
  225.7 0.0 all-gather.5.cloned.1.call-update
  225.7 0.0 reduce-scatter.5.cloned.1.call-start
  225.8 79.4 %all-gather.5.cloned.1.call-done = bf16[1024,2048]{1,0:T(8,128)(2,1)} async-done(((bf16[256,2048]{1,0:T(8,128)(2,1)}), bf16[1024,2048]{1,0:T(8,128)(2,1)}) %all-gather.5.cloned.1.call-update) | async-done | bytes 4194320 | tf_op jit(solution)/shard_map/all_gather | solution.py:21
  305.2 0.0 copy-done
  305.2 3.5 %fusion.1 = f32[1024,256]{1,0:T(8,128)S(1)} fusion(bf16[1024,2048]{1,0:T(8,128)(2,1)} %all-gather.5.cloned.1.call-done, bf16[256,2048]{1,0:T(8,128)(2,1)S(1)} %copy-done), kind=kOutput, calls=%fused_computation.1 | convolution fusion | flops 1073741824 | bytes 6291456 | tf_op jit(solution)/shard_map/dot_general | solution.py:20
  308.7 1.0 copy.4
  309.7 0.0 reduce-scatter.5.cloned.1.call-update
  309.7 23.6 %reduce-scatter.5.cloned.1.call-done = f32[256,256]{1,0:T(8,128)} async-done(((f32[1024,256]{1,0:T(8,128)}), f32[256,256]{1,0:T(8,128)}) %reduce-scatter.5.cloned.1.call-update) | async-done | bytes 262160 | tf_op jit(solution)/shard_map/reduce_scatter | solution.py:32
Async XLA Ops:
  6.5 298.7 %copy-start = (bf16[256,2048]{1,0:T(8,128)(2,1)S(1)}, bf16[256,2048]{1,0:T(8,128)(2,1)}, u32[]{:S(2)}) copy-start(bf16[256,2048]{1,0:T(8,128)(2,1)} %param.4) | copy-start | bytes 3145732
  6.5 85.3 %all-gather.3.cloned.1.call-start = ((), (), s32[]{:S(2)}) async-start(), calls=%async_computation.4 | async-start | bytes 5242880 | tf_op jit(solution)/shard_map/all_gather | solution.py:8
  7.3 169.4 %reduce-scatter.3.cloned.1.call-start = ((), (), s32[]{:S(2)}) async-start(), calls=%async_computation.5 | async-start | bytes 10485760 | tf_op jit(solution)/shard_map/reduce_scatter | solution.py:10
  106.3 198.9 %all-gather.5.cloned.1.call-start = ((), (), s32[]{:S(2)}) async-start(), calls=%async_computation.6 | async-start | bytes 5242880 | tf_op jit(solution)/shard_map/all_gather | solution.py:21
  225.7 107.6 %reduce-scatter.5.cloned.1.call-start = ((), (), s32[]{:S(2)}) async-start(), calls=%async_computation.7 | async-start | bytes 1310720 | tf_op jit(solution)/shard_map/reduce_scatter | solution.py:32
Sparse Core Ops, SparseCore 0:
  8.9 82.8 all-gather.2
  106.4 70.1 reduce-scatter.2
  225.9 79.2 all-gather.4
  309.9 23.4 reduce-scatter.4
where the time goes:
time: 341 us; the launch traced here: 340 us
  waiting for transfers between devices  259 us (76%)
  blocking collectives  47.4 us (14%)
  matrix products  17.9 us (5%)
  between operations  13.1 us (4%)
    all_gather x1, waiting for transfers between devices, local(): all_rows = lax.all_gather(test_features, 'blk', axis=0, tiled=True)  84.5 us
    all_gather x1, waiting for transfers between devices, local(): lax.all_gather(preconditioned, 'blk', axis=0, tiled=True)  79.4 us
    reduce_scatter x1, waiting for transfers between devices, local(): lax.psum_scatter(slab_terms, 'panel', scatter_dimension=0, tiled=True)  70.3 us
    all_to_all x1, blocking collectives, local(): lax.all_to_all(reduced, 'blk', split_axis=0, concat_axis=1, tiled=True)  29 us
    reduce_scatter x1, waiting for transfers between devices, local(): lax.psum_scatter(partial_scores, 'panel', scatter_dimension=0, tiled=True)  23.6 us
    all_to_all x1, blocking collectives, local(): lax.all_to_all(lax.all_to_all(reduced, 'blk', split_axis=0, concat_axis=1...  18.4 us
    dot_general x1, matrix products, local(): jnp.dot(all_rows, kernel_inverse, preferred_element_type=jnp.float32)  14.4 us
  transfers between devices with their start and end apart: 4, of which 4 were waited for; matrix products, arithmetic and copies ran while one was open for 0% of the time, Pallas kernels for 0%

commit v1 on v0

--- a/solution.py
+++ b/solution.py
@@ -1,7 +1,14 @@
+import functools
+
 import jax
 import jax.numpy as jnp
 from jax import lax
+from jax.experimental import pallas as pl
+from jax.experimental.pallas import tpu as pltpu
 from jax.sharding import PartitionSpec as P
+
+MESH = pl.DeviceIdType.MESH
+VMEM_BYTES = 56 * 1024 * 1024
 
 
 def local(test_features, train_features, kernel_inverse):
@@ -32,7 +39,333 @@
     return lax.psum_scatter(partial_scores, "panel", scatter_dimension=0, tiled=True)
 
 
+def kernel(
+    n, tile, t_ref, r_ref, k_ref, out_ref,
+    tbuf, rbuf, stage, kbuf, sbuf, crecv, xrecv, zrecv,
+    lsem, tsend, trecv, rsend, rrecv, gsend, grecv, csend, crsem, xsend, xrsem, zsend, zrsem,
+):
+    rows, depth = t_ref.shape
+    half = rows // 2
+    g = lax.axis_index("groups")
+    b = lax.axis_index("blk")
+    p = lax.axis_index("panel")
+    sib = p + 1 - 2 * lax.rem(p, 2)
+    peer = lax.rem(p + 2, 4)
+
+    def at(blk, panel):
+        return (g, blk, panel)
+
+    def remote(src, dst, send, recv, blk, panel):
+        return pltpu.make_async_remote_copy(
+            src_ref=src, dst_ref=dst, send_sem=send, recv_sem=recv,
+            device_id=at(blk, panel), device_id_type=MESH,
+        )
+
+    barrier = pltpu.get_barrier_semaphore()
+    for k in range(1, n):
+        pl.semaphore_signal(barrier, inc=1, device_id=at(lax.rem(b + k, n), p), device_id_type=MESH)
+    pl.semaphore_signal(barrier, inc=1, device_id=at(b, sib), device_id_type=MESH)
+    pl.semaphore_signal(barrier, inc=1, device_id=at(b, peer), device_id_type=MESH)
+
+    load_k = pltpu.make_async_copy(k_ref, kbuf, lsem.at[0])
+    load_t = pltpu.make_async_copy(t_ref, tbuf.at[b], lsem.at[1])
+    load_r = pltpu.make_async_copy(r_ref, rbuf.at[b], lsem.at[2])
+    pl.semaphore_wait(barrier, n + 1)
+
+    diag = b == p
+    across = b == peer
+    entry = lax.rem(b, 2) == lax.rem(p, 2)
+    top = pl.ds(0, half)
+    low = pl.ds(half, half)
+
+    own_top = remote(r_ref.at[top], rbuf.at[b, top], rsend.at[0], rrecv.at[b, 0], p, p)
+    own_low = remote(r_ref.at[low], stage, rsend.at[1], grecv, b, peer)
+    own_peer = remote(r_ref, rbuf.at[b], rsend.at[0], rrecv.at[b, 0], b, peer)
+    own_sib = remote(r_ref, rbuf.at[b], rsend.at[1], rrecv.at[b, 0], b, sib)
+
+    @pl.when(jnp.logical_not(diag))
+    def _():
+        own_low.start()
+        own_top.start()
+
+    @pl.when(diag)
+    def _():
+        own_peer.start()
+        own_sib.start()
+
+    def t_copy(src, c, way, blk):
+        return remote(src, tbuf.at[c], tsend.at[way, c], trecv.at[c], blk, p)
+
+    @pl.when(b > 0)
+    def _():
+        t_copy(t_ref, b, 0, b - 1).start()
+
+    @pl.when(b < n - 1)
+    def _():
+        t_copy(t_ref, b, 1, b + 1).start()
+
+    load_t.start()
+    load_k.start()
+
+    @pl.when(diag)
+    def _():
+        load_r.start()
+
+    go_on = remote(stage, rbuf.at[b, low], gsend, rrecv.at[b, 1], peer, p)
+
+    @pl.when(jnp.logical_not(across))
+    def _():
+        remote(stage, stage, gsend, grecv, b, peer).wait_recv()
+        go_on.start()
+
+    def r_part(j, which):
+        start = pl.multiple_of(which * half, half)
+        return rbuf.at[j, pl.ds(start, half)]
+
+    def r_move(j, which, way, panel):
+        return remote(
+            r_part(j, which), r_part(j, which), rsend.at[2 + j * 4 + way],
+            rrecv.at[j, which], b, panel,
+        )
+
+    mine = jnp.where(diag, 0, 1)
+
+    @pl.when(entry)
+    def _():
+        @pl.when(across)
+        def _():
+            remote(rbuf.at[b], rbuf.at[b], rsend.at[0], rrecv.at[b, 0], b, peer).wait_recv()
+            remote(rbuf.at[b], rbuf.at[b], rsend.at[2 + 4 * n], rrecv.at[b, 0], b, sib).start()
+
+        for k in (1, n - 1, 2):
+            j = lax.rem(b + k, n)
+            r_move(j, mine, 0, peer).wait_recv()
+            r_move(j, mine, 0, peer).start()
+            r_move(j, mine, 1, sib).start()
+
+    def arrive(c, blk, way, more):
+        t_copy(tbuf.at[c], c, way, blk).wait_recv()
+
+        @pl.when(more)
+        def _():
+            t_copy(tbuf.at[c], c, way, blk).start()
+
+    def arrivals(k):
+        @pl.when(b - k >= 0)
+        def _():
+            arrive(b - k, lax.rem(b + 1, n), 1, b < n - 1)
+
+        @pl.when(b + k < n)
+        def _():
+            arrive(b + k, lax.rem(b + n - 1, n), 0, b > 0)
+
+    def compute(c):
+        sbuf[c] = jnp.zeros_like(sbuf[c])
+
+        def step(t, carry):
+            cols = pl.ds(pl.multiple_of(t * tile, tile), tile)
+            part = jnp.dot(tbuf[c], kbuf[:, cols], preferred_element_type=jnp.float32)
+            hi = part.astype(jnp.bfloat16)
+            lo = (part - hi.astype(jnp.float32)).astype(jnp.bfloat16)
+            for j in range(n):
+                right = rbuf[j, :, cols]
+                dims = (((1,), (1,)), ((), ()))
+                sbuf[c, j] += lax.dot_general(
+                    hi, right, dims, preferred_element_type=jnp.float32
+                ) + lax.dot_general(lo, right, dims, preferred_element_type=jnp.float32)
+            return carry
+
+        lax.fori_loop(0, depth // tile, step, 0)
+
+        other = lax.rem(c, 2) != lax.rem(p, 2)
+        copy = remote(sbuf.at[c], crecv.at[c], csend.at[c], crsem.at[c], b, sib)
+
+        @pl.when(other)
+        def _():
+            copy.start()
+
+        @pl.when(jnp.logical_not(other))
+        def _():
+            copy.wait_recv()
+            sbuf[c] += crecv[c]
+
+            @pl.when(c != p)
+            def _():
+                remote(sbuf.at[c], xrecv, xsend, xrsem, b, peer).start()
+
+    def z_copy(k):
+        to = lax.rem(b + k, n)
+        return remote(sbuf.at[p, to], zrecv.at[b], zsend.at[k - 1], zrsem.at[b], to, p)
+
+    def spread(c):
+        @pl.when(c == p)
+        def _():
+            remote(sbuf.at[c], xrecv, xsend, xrsem, b, peer).wait_recv()
+            sbuf[c] += xrecv[...]
+            for k in range(1, n):
+                z_copy(k).start()
+
+    def at_step(k, f):
+        @pl.when(b - k >= 0)
+        def _():
+            f(b - k)
+
+        @pl.when(b + k < n)
+        def _():
+            f(b + k)
+
+    arrivals(1)
+
+    @pl.when(entry)
+    def _():
+        for k in (1, n - 1, 2):
+            j = lax.rem(b + k, n)
+            r_move(j, 1 - mine, 0, peer).wait_recv()
+            r_move(j, 1 - mine, 2, sib).start()
+
+    @pl.when(jnp.logical_not(entry))
+    def _():
+        remote(rbuf.at[b], rbuf.at[b], rsend.at[0], rrecv.at[b, 0], b, sib).wait_recv()
+        for k in (1, n - 1, 2):
+            j = lax.rem(b + k, n)
+            r_move(j, 0, 0, sib).wait_recv()
+            r_move(j, 1, 0, sib).wait_recv()
+
+    load_t.wait()
+    load_k.wait()
+
+    @pl.when(diag)
+    def _():
+        load_r.wait()
+
+    compute(b)
+    for k in range(1, n):
+        if k > 1:
+            arrivals(k)
+        at_step(k, compute)
+        if k == 1:
+            spread(b)
+        else:
+            at_step(k - 1, spread)
+    at_step(n - 1, spread)
+
+    total = sbuf[p, b]
+    for k in range(1, n):
+        j = lax.rem(b + k, n)
+        remote(zrecv.at[j], zrecv.at[j], zsend.at[k - 1], zrsem.at[j], j, p).wait_recv()
+        total = total + zrecv[j]
+    out_ref[...] = total
+
+    @pl.when(jnp.logical_not(diag))
+    def _():
+        own_top.wait_send()
+        own_low.wait_send()
+
+    @pl.when(diag)
+    def _():
+        own_peer.wait_send()
+        own_sib.wait_send()
+
+    @pl.when(b > 0)
+    def _():
+        t_copy(t_ref, b, 0, b - 1).wait_send()
+
+    @pl.when(b < n - 1)
+    def _():
+        t_copy(t_ref, b, 1, b + 1).wait_send()
+
+    @pl.when(jnp.logical_not(across))
+    def _():
+        go_on.wait_send()
+
+    @pl.when(entry)
+    def _():
+        @pl.when(across)
+        def _():
+            remote(rbuf.at[b], rbuf.at[b], rsend.at[2 + 4 * n], rrecv.at[b, 0], b, sib).wait_send()
+
+        for k in range(1, n):
+            j = lax.rem(b + k, n)
+            r_move(j, mine, 0, peer).wait_send()
+            r_move(j, mine, 1, sib).wait_send()
+            r_move(j, 1 - mine, 2, sib).wait_send()
+
+    for k in range(1, n):
+        @pl.when(jnp.logical_and(b - k >= 0, b < n - 1))
+        def _():
+            t_copy(tbuf.at[b - k], b - k, 1, b + 1).wait_send()
+
+        @pl.when(jnp.logical_and(b + k < n, b > 0))
+        def _():
+            t_copy(tbuf.at[b + k], b + k, 0, b - 1).wait_send()
+
+    for c in range(n):
+        @pl.when(c % 2 != lax.rem(p, 2))
+        def _():
+            remote(sbuf.at[c], crecv.at[c], csend.at[c], crsem.at[c], b, sib).wait_send()
+
+    remote(sbuf.at[peer], xrecv, xsend, xrsem, b, peer).wait_send()
+    for k in range(1, n):
+        z_copy(k).wait_send()
+
+
+def fused(n, test_features, train_features, kernel_inverse):
+    rows, depth = test_features.shape
+    bf16, f32 = jnp.bfloat16, jnp.float32
+    dma = pltpu.SemaphoreType.DMA
+    return pl.pallas_call(
+        functools.partial(kernel, n, min(512, depth)),
+        out_shape=jax.ShapeDtypeStruct((rows, rows), f32),
+        in_specs=[pl.BlockSpec(memory_space=pl.ANY)] * 3,
+        out_specs=pl.BlockSpec(memory_space=pltpu.VMEM),
+        scratch_shapes=[
+            pltpu.VMEM((n, rows, depth), bf16),
+            pltpu.VMEM((n, rows, depth), bf16),
+            pltpu.VMEM((rows // 2, depth), bf16),
+            pltpu.VMEM((depth, depth), bf16),
+            pltpu.VMEM((n, n, rows, rows), f32),
+            pltpu.VMEM((n, n, rows, rows), f32),
+            pltpu.VMEM((n, rows, rows), f32),
+            pltpu.VMEM((n, rows, rows), f32),
+            dma((3,)),
+            dma((2, n)),
+            dma((n,)),
+            dma((3 + 4 * n,)),
+            dma((n, 2)),
+            dma,
+            dma,
+            dma((n,)),
+            dma((n,)),
+            dma,
+            dma,
+            dma((n,)),
+            dma((n,)),
+        ],
+        compiler_params=pltpu.CompilerParams(
+            collective_id=0, has_side_effects=True, vmem_limit_bytes=VMEM_BYTES
+        ),
+        cost_estimate=pl.CostEstimate(
+            flops=2 * n * rows * depth * (depth + 2 * n * rows),
+            bytes_accessed=2 * depth * (depth + 2 * rows) + 4 * rows * rows,
+            transcendentals=0,
+        ),
+    )(test_features, train_features, kernel_inverse)
+
+
+def held_bytes(n, rows, depth):
+    return 4 * n * rows * depth + 2 * depth * depth + 8 * n * rows * n * rows
+
+
 def solution(mesh):
     in_specs = (P(("groups", "blk"), "panel"), P(("groups", "blk"), "panel"), P("panel", "blk"))
     out_specs = P(("groups", "panel"), "blk")
-    return jax.shard_map(local, mesh=mesh, in_specs=in_specs, out_specs=out_specs, check_vma=False)
+    blocks, panels = mesh.shape["blk"], mesh.shape["panel"]
+
+    def run(test_features, train_features, kernel_inverse):
+        rows, depth = test_features.shape
+        same = train_features.shape == (rows, depth) and kernel_inverse.shape == (depth, depth)
+        if blocks == 4 and panels == 4 and same and held_bytes(blocks, rows, depth) < VMEM_BYTES * 3 // 4:
+            return fused(blocks, test_features, train_features, kernel_inverse)
+        return local(test_features, train_features, kernel_inverse)
+
+    return jax.shard_map(run, mesh=mesh, in_specs=in_specs, out_specs=out_specs, check_vma=False)

time: 341 us -> 157 us (0.46)
  the two profiles are of different devices: /device:TPU:1 before, /device:TPU:27 now
where the time goes in v1:
time: 157 us
  Pallas kernels  155 us (99%)
  local copies, waits for them, and re-layouts  1.67 us (1%)
    pallas_call x1, Pallas kernels, fused(): pl.pallas_call(functools.partial(kernel, n, min(512, depth)), out_shape=j...  155 us

profile of v1, /device:TPU:27, one launch (start us, length us, event | category | flops | bytes accessed | tf_op | source)
XLA Modules:
  0.0 156.8 jit_solution(2966888521132678234)
XLA Ops:
  0.0 155.1 %shard_map.37 = f32[256,256]{1,0:T(8,128)} custom-call(bf16[256,2048]{1,0:T(8,128)(2,1)} %t_ref.1, bf16[256,2048]{1,0:T(8,128)(2,1)} %r_ref.1, bf16[2048,2048]{1,0:T(8,128)(2,1)} %k_ref.1), custom_call_target="tpu_custom_call" | custom-call | flops 17179869184 | bytes 10747904 | tf_op jit(solution)/shard_map/pallas_call | solution.py:316
  155.1 1.7 %copy.5 = f32[256,256]{1,0:T(8,128)} copy(f32[256,256]{1,0:T(8,128)} %shard_map.37) | data formatting | bytes 524288

commit v2 on v0

--- a/solution.py
+++ b/solution.py
@@ -1,7 +1,14 @@
+import functools
+
 import jax
 import jax.numpy as jnp
 from jax import lax
+from jax.experimental import pallas as pl
+from jax.experimental.pallas import tpu as pltpu
 from jax.sharding import PartitionSpec as P
+
+MESH = pl.DeviceIdType.MESH
+VMEM_BYTES = 56 * 1024 * 1024
 
 
 def local(test_features, train_features, kernel_inverse):
@@ -32,7 +39,374 @@
     return lax.psum_scatter(partial_scores, "panel", scatter_dimension=0, tiled=True)
 
 
+def kernel(
+    n, tile, t_ref, r_ref, k_ref, out_ref,
+    tbuf, rbuf, tmore, rmore, stage, kbuf, sbuf, crecv, xrecv, zrecv, fbuf, home,
+    lsem, tsend, trecv, msend, mrecv, rsend, rrecv, qsend, qrecv, gsend, grecv,
+    csend, crsem, xsend, xrsem, zsend, zrsem, fsend, frsem,
+):
+    rows, depth = t_ref.shape
+    half, quarter = rows // 2, rows // 4
+    g = lax.axis_index("groups")
+    b = lax.axis_index("blk")
+    p = lax.axis_index("panel")
+    core, chip = lax.rem(p, 2), p // 2
+    sib = p + 1 - 2 * core
+    peer = lax.rem(p + 2, 4)
+    far = peer + 1 - 2 * core
+
+    def at(blk, panel):
+        return (g, blk, panel)
+
+    def remote(src, dst, send, recv, blk, panel):
+        return pltpu.make_async_remote_copy(
+            src_ref=src, dst_ref=dst, send_sem=send, recv_sem=recv,
+            device_id=at(blk, panel), device_id_type=MESH,
+        )
+
+    def on(condition, f, *args):
+        @pl.when(condition)
+        def _():
+            f(*args)
+
+    def both(*conditions):
+        return functools.reduce(jnp.logical_and, conditions)
+
+    barrier = pltpu.get_barrier_semaphore()
+    partners = [at(lax.rem(b + k, n), p) for k in range(1, n)]
+    partners += [at(b, sib), at(b, peer), at(b, far)]
+    for partner in partners:
+        pl.semaphore_signal(barrier, inc=1, device_id=partner, device_id_type=MESH)
+    load_k = pltpu.make_async_copy(k_ref, kbuf, lsem.at[0])
+    load_t = pltpu.make_async_copy(t_ref, tbuf.at[b], lsem.at[1])
+    load_r = pltpu.make_async_copy(r_ref, rbuf.at[b], lsem.at[2])
+    load_m = pltpu.make_async_copy(r_ref, rmore.at[b], lsem.at[2])
+    pl.semaphore_wait(barrier, n + 2)
+
+    diag = b == p
+    outer = jnp.logical_or(p == 0, p == 3)
+    helper_blk = jnp.where(p == 0, 1, 2)
+    helper = both(outer, b == helper_blk)
+    giver = both(jnp.logical_not(outer), diag)
+    first = jnp.where(p == 1, 1, 0)
+    last = jnp.where(p == 2, n - 2, n - 1)
+    active = both(b >= first, b <= last)
+    go_left, go_right = both(b - 1 >= first, b > 0), both(b + 1 <= last, b < n - 1)
+    left, right = lax.rem(b + n - 1, n), lax.rem(b + 1, n)
+    entry_panel = 3 * lax.rem(b, 2)
+    entry = p == entry_panel
+    entry_peer = peer == entry_panel
+    staged = both(outer, b != peer)
+
+    r_stage = remote(r_ref, stage, rsend.at[0], grecv, b, peer)
+    r_more = remote(r_ref, rmore.at[b], rsend.at[0], qrecv.at[b], helper_blk, p)
+    r_end = remote(r_ref, rbuf.at[b], rsend.at[0], rrecv.at[b], p, p)
+    r_peer = remote(r_ref, rbuf.at[b], rsend.at[1], rrecv.at[b], b, peer)
+    r_sib = remote(r_ref, rbuf.at[b], rsend.at[2], rrecv.at[b], b, sib)
+    stages = both(jnp.logical_not(outer), jnp.logical_not(diag))
+    mores = both(outer, b != helper_blk)
+    on(stages, r_stage.start)
+    on(mores, r_more.start)
+    on(helper, r_end.start)
+    on(diag, r_peer.start)
+    on(diag, r_sib.start)
+
+    def t_copy(src, c, way):
+        return remote(src, tbuf.at[c], tsend.at[way, c], trecv.at[c], right if way else left, p)
+
+    def t_more(src, c):
+        return remote(src, tmore.at[c], msend.at[c], mrecv.at[c], b, sib)
+
+    on(go_left, t_copy(t_ref, b, 0).start)
+    on(go_right, t_copy(t_ref, b, 1).start)
+    load_t.start()
+    load_k.start()
+    on(diag, load_r.start)
+    on(helper, load_m.start)
+    on(giver, t_more(t_ref, b).start)
+
+    r_on = remote(stage, rbuf.at[b], gsend, rrecv.at[b], peer, p)
+
+    @pl.when(staged)
+    def _():
+        r_stage.wait_recv()
+        r_on.start()
+
+    def r_move(j, way):
+        to = peer if way == 0 else sib
+        return remote(rbuf.at[j], rbuf.at[j], rsend.at[3 + 2 * j + way], rrecv.at[j], b, to)
+
+    def r_pass(j):
+        return remote(rmore.at[j], rbuf.at[j], qsend.at[j], rrecv.at[j], p, p)
+
+    def arrivals(k):
+        def arrive(c, way, more):
+            t_copy(tbuf.at[c], c, way).wait_recv()
+            on(more, t_copy(tbuf.at[c], c, way).start)
+            on(giver, t_more(tbuf.at[c], c).start)
+
+        on(both(b - k >= 0, b <= last), arrive, b - k, 1, go_right)
+        on(both(b + k < n, b >= first), arrive, b + k, 0, go_left)
+
+    def more_arrives(j):
+        remote(rmore.at[j], rmore.at[j], qsend.at[j], qrecv.at[j], b, p).wait_recv()
+        on(j != p, r_pass(j).start)
+
+    def entry_arrives(j):
+        r_move(j, 0).wait_recv()
+        r_move(j, 0).start()
+        r_move(j, 1).start()
+
+    def peer_arrives(j):
+        r_move(j, 1).wait_recv()
+        r_move(j, 1).start()
+
+    near = [lax.rem(b + k, n) for k in (1, n - 1, 2)]
+
+    def compute(c):
+        sbuf[c] = jnp.zeros_like(sbuf[c])
+        dims = (((1,), (1,)), ((), ()))
+
+        def add(part, train, cols):
+            hi = part.astype(jnp.bfloat16)
+            lo = (part - hi.astype(jnp.float32)).astype(jnp.bfloat16)
+            for j in range(n):
+                block = train[j, :, cols]
+                sbuf[c, j] += lax.dot_general(
+                    hi, block, dims, preferred_element_type=jnp.float32
+                ) + lax.dot_general(lo, block, dims, preferred_element_type=jnp.float32)
+
+        def step(t, carry):
+            cols = pl.ds(pl.multiple_of(t * tile, tile), tile)
+            add(jnp.dot(tbuf[c], kbuf[:, cols], preferred_element_type=jnp.float32), rbuf, cols)
+            return carry
+
+        def step_more(t, carry):
+            cols = pl.ds(pl.multiple_of(t * tile, tile), tile)
+            part = lax.dot_general(
+                tmore[c], kbuf[cols, :], dims, preferred_element_type=jnp.float32
+            )
+            add(part, rmore, cols)
+            return carry
+
+        @pl.when(active)
+        def _():
+            lax.fori_loop(0, depth // tile, step, 0)
+
+        @pl.when(helper)
+        def _():
+            t_more(tmore.at[c], c).wait_recv()
+            lax.fori_loop(0, depth // tile, step_more, 0)
+
+        core_copy(c).start()
+
+    def span(start, size):
+        return pl.ds(pl.multiple_of(start, quarter), size)
+
+    own_half = span(core * half, half)
+    sib_half = span((1 - core) * half, half)
+    own_part = span(core * half + chip * quarter, quarter)
+    peer_part = span(core * half + (1 - chip) * quarter, quarter)
+
+    def core_copy(c):
+        return remote(sbuf.at[c, :, sib_half], crecv.at[c], csend.at[c], crsem.at[c], b, sib)
+
+    def chip_copy(c):
+        return remote(sbuf.at[c, :, peer_part], xrecv.at[c], xsend.at[c], xrsem.at[c], b, peer)
+
+    def plane_copy(c, k):
+        to = lax.rem(b + k, n)
+        return remote(
+            sbuf.at[c, to, own_part], zrecv.at[b, c], zsend.at[c, k - 1], zrsem.at[b, c], to, p
+        )
+
+    def join_cores(c):
+        core_copy(c).wait_recv()
+        sbuf[c, :, own_half] += crecv[c]
+        chip_copy(c).start()
+
+    def join_chips(c):
+        chip_copy(c).wait_recv()
+        sbuf[c, :, own_part] += xrecv[c]
+        for k in range(1, n):
+            plane_copy(c, k).start()
+
+    def at_step(k, f):
+        if k == 0:
+            f(b)
+        else:
+            on(b - k >= 0, f, b - k)
+            on(b + k < n, f, b + k)
+
+    arrivals(1)
+
+    @pl.when(helper)
+    def _():
+        for j in near:
+            more_arrives(j)
+
+    @pl.when(entry)
+    def _():
+        for j in near:
+            entry_arrives(j)
+        on(jnp.logical_not(diag), peer_arrives, b)
+
+    arrivals(2)
+
+    @pl.when(entry_peer)
+    def _():
+        on(jnp.logical_not(diag), peer_arrives, b)
+        for j in near:
+            peer_arrives(j)
+
+    @pl.when(jnp.logical_not(jnp.logical_or(entry, entry_peer)))
+    def _():
+        for j in range(n):
+            r_move(j, 1).wait_recv()
+
+    load_t.wait()
+    load_k.wait()
+    on(diag, load_r.wait)
+    on(helper, load_m.wait)
+
+    for k in range(n):
+        if k > 2:
+            arrivals(k)
+        at_step(k, compute)
+        at_step(k, join_cores)
+        if k > 0:
+            at_step(k - 1, join_chips)
+    at_step(n - 1, join_chips)
+
+    def home_copy(c):
+        return remote(fbuf.at[c], home.at[p], fsend.at[c], frsem.at[p], b, c)
+
+    for c in range(n):
+        total = sbuf[c, b, own_part]
+        for k in range(1, n):
+            j = lax.rem(b + k, n)
+            remote(zrecv.at[j, c], zrecv.at[j, c], zsend.at[c, 0], zrsem.at[j, c], j, p).wait_recv()
+            total = total + zrecv[j, c]
+        fbuf[c] = total
+        on(p != c, home_copy(c).start)
+    out_ref[own_part, :] = fbuf[p]
+    for q in range(n):
+        @pl.when(p != q)
+        def _():
+            remote(home.at[q], home.at[q], fsend.at[q], frsem.at[q], b, q).wait_recv()
+            start = (q % 2) * half + (q // 2) * quarter
+            out_ref[start:start + quarter, :] = home[q]
+
+    on(stages, r_stage.wait_send)
+    on(mores, r_more.wait_send)
+    on(helper, r_end.wait_send)
+    on(diag, r_peer.wait_send)
+    on(diag, r_sib.wait_send)
+    on(go_left, t_copy(t_ref, b, 0).wait_send)
+    on(go_right, t_copy(t_ref, b, 1).wait_send)
+    on(giver, t_more(t_ref, b).wait_send)
+    on(staged, r_on.wait_send)
+
+    @pl.when(helper)
+    def _():
+        for j in near:
+            on(j != p, r_pass(j).wait_send)
+
+    @pl.when(entry)
+    def _():
+        for j in near:
+            r_move(j, 0).wait_send()
+            r_move(j, 1).wait_send()
+        on(jnp.logical_not(diag), r_move(b, 1).wait_send)
+
+    @pl.when(entry_peer)
+    def _():
+        for j in near:
+            r_move(j, 1).wait_send()
+        on(jnp.logical_not(diag), r_move(b, 1).wait_send)
+
+    def t_left_all(c, way, more):
+        on(more, t_copy(tbuf.at[c], c, way).wait_send)
+        on(giver, t_more(tbuf.at[c], c).wait_send)
+
+    for k in range(1, n):
+        on(both(b - k >= 0, b <= last), t_left_all, b - k, 1, go_right)
+        on(both(b + k < n, b >= first), t_left_all, b + k, 0, go_left)
+    for c in range(n):
+        core_copy(c).wait_send()
+        chip_copy(c).wait_send()
+        for k in range(1, n):
+            plane_copy(c, k).wait_send()
+        on(p != c, home_copy(c).wait_send)
+
+
+def fused(n, test_features, train_features, kernel_inverse):
+    rows, depth = test_features.shape
+    bf16, f32 = jnp.bfloat16, jnp.float32
+    dma = pltpu.SemaphoreType.DMA
+    return pl.pallas_call(
+        functools.partial(kernel, n, min(512, depth)),
+        out_shape=jax.ShapeDtypeStruct((rows, rows), f32),
+        in_specs=[pl.BlockSpec(memory_space=pl.ANY)] * 3,
+        out_specs=pl.BlockSpec(memory_space=pltpu.VMEM),
+        scratch_shapes=[
+            pltpu.VMEM((n, rows, depth), bf16),
+            pltpu.VMEM((n, rows, depth), bf16),
+            pltpu.VMEM((n, rows, depth), bf16),
+            pltpu.VMEM((n, rows, depth), bf16),
+            pltpu.VMEM((rows, depth), bf16),
+            pltpu.VMEM((depth, depth), bf16),
+            pltpu.VMEM((n, n, rows, rows), f32),
+            pltpu.VMEM((n, n, rows // 2, rows), f32),
+            pltpu.VMEM((n, n, rows // 4, rows), f32),
+            pltpu.VMEM((n, n, rows // 4, rows), f32),
+            pltpu.VMEM((n, rows // 4, rows), f32),
+            pltpu.VMEM((n, rows // 4, rows), f32),
+            dma((3,)),
+            dma((2, n)),
+            dma((n,)),
+            dma((n,)),
+            dma((n,)),
+            dma((3 + 2 * n,)),
+            dma((n,)),
+            dma((n,)),
+            dma((n,)),
+            dma,
+            dma,
+            dma((n,)),
+            dma((n,)),
+            dma((n,)),
+            dma((n,)),
+            dma((n, n - 1)),
+            dma((n, n)),
+            dma((n,)),
+            dma((n,)),
+        ],
+        compiler_params=pltpu.CompilerParams(
+            collective_id=0, has_side_effects=True, vmem_limit_bytes=VMEM_BYTES
+        ),
+        cost_estimate=pl.CostEstimate(
+            flops=2 * n * rows * depth * (depth + 2 * n * rows),
+            bytes_accessed=2 * depth * (depth + 2 * rows) + 4 * rows * rows,
+            transcendentals=0,
+        ),
+    )(test_features, train_features, kernel_inverse)
+
+
+def held_bytes(n, rows, depth):
+    return 8 * n * rows * depth + 2 * depth * depth + 8 * n * rows * n * rows
+
+
 def solution(mesh):
     in_specs = (P(("groups", "blk"), "panel"), P(("groups", "blk"), "panel"), P("panel", "blk"))
     out_specs = P(("groups", "panel"), "blk")
-    return jax.shard_map(local, mesh=mesh, in_specs=in_specs, out_specs=out_specs, check_vma=False)
+    blocks, panels = mesh.shape["blk"], mesh.shape["panel"]
+
+    def run(test_features, train_features, kernel_inverse):
+        rows, depth = test_features.shape
+        same = train_features.shape == (rows, depth) and kernel_inverse.shape == (depth, depth)
+        if blocks == 4 and panels == 4 and same and held_bytes(blocks, rows, depth) < VMEM_BYTES * 3 // 4:
+            return fused(blocks, test_features, train_features, kernel_inverse)
+        return local(test_features, train_features, kernel_inverse)
+
+    return jax.shard_map(run, mesh=mesh, in_specs=in_specs, out_specs=out_specs, check_vma=False)

time: 341 us -> 188 us (0.55)
  waiting for transfers between devices: 259 us -> 0 us
  Pallas kernels: 0 us -> 186 us
  blocking collectives: 47.4 us -> 0 us
  matrix products: 17.9 us -> 0 us
  between operations: 13.1 us -> 0.01 us
    pallas_call x0 -> x1, Pallas kernels: none -> 186 us  [fused(): pl.pallas_call(functools.partial(kernel, n, min(512, depth)), out_shape=j...]
    all_gather x2 -> x0, waiting for transfers between devices: 164 us -> none  [the longest x1 84.5 us: local(): all_rows = lax.all_gather(test_features, 'blk', axis=0, tiled=True)]
    reduce_scatter x2 -> x0, waiting for transfers between devices: 93.9 us -> none  [the longest x1 70.3 us: local(): lax.psum_scatter(slab_terms, 'panel', scatter_dimension=0, tiled=True)]
    all_to_all x2 -> x0, blocking collectives: 47.4 us -> none  [the longest x1 29 us: local(): lax.all_to_all(reduced, 'blk', split_axis=0, concat_axis=1, tiled=True)]
    dot_general x2 -> x0, matrix products: 17.9 us -> none  [the longest x1 14.4 us: local(): jnp.dot(all_rows, kernel_inverse, preferred_element_type=jnp.float32)]
  transfers between devices with their start and end apart: 4 -> 0, of which waited for: 4 -> 0; matrix products, arithmetic and copies ran while one was open for 0% -> 0% of each run, Pallas kernels for 0% -> 0%
where the time goes in v2:
time: 188 us
  Pallas kernels  186 us (99%)
    pallas_call x1, Pallas kernels, fused(): pl.pallas_call(functools.partial(kernel, n, min(512, depth)), out_shape=j...  186 us

profile of v2, /device:TPU:1, one launch (start us, length us, event | category | flops | bytes accessed | tf_op | source)
XLA Modules:
  0.0 187.9 jit_solution(4794964968019878198)
XLA Ops:
  0.0 186.3 %shard_map.37 = f32[256,256]{1,0:T(8,128)} custom-call(bf16[256,2048]{1,0:T(8,128)(2,1)} %t_ref.1, bf16[256,2048]{1,0:T(8,128)(2,1)} %r_ref.1, bf16[2048,2048]{1,0:T(8,128)(2,1)} %k_ref.1), custom_call_target="tpu_custom_call" | custom-call | flops 17179869184 | bytes 10747904 | tf_op jit(solution)/shard_map/pallas_call | solution.py:347
  186.3 1.7 copy.5

commit v3 on v2

--- a/solution.py
+++ b/solution.py
@@ -41,8 +41,8 @@
 
 def kernel(
     n, tile, t_ref, r_ref, k_ref, out_ref,
-    tbuf, rbuf, tmore, rmore, stage, kbuf, sbuf, crecv, xrecv, zrecv, fbuf, home,
-    lsem, tsend, trecv, msend, mrecv, rsend, rrecv, qsend, qrecv, gsend, grecv,
+    tbuf, rbuf, stage, kbuf, pbuf, sbuf, crecv, xrecv, zrecv, fbuf, home,
+    lsem, tsend, trecv, rsend, rrecv, gsend, grecv,
     csend, crsem, xsend, xrsem, zsend, zrsem, fsend, frsem,
 ):
     rows, depth = t_ref.shape
@@ -80,124 +80,92 @@
     load_k = pltpu.make_async_copy(k_ref, kbuf, lsem.at[0])
     load_t = pltpu.make_async_copy(t_ref, tbuf.at[b], lsem.at[1])
     load_r = pltpu.make_async_copy(r_ref, rbuf.at[b], lsem.at[2])
-    load_m = pltpu.make_async_copy(r_ref, rmore.at[b], lsem.at[2])
     pl.semaphore_wait(barrier, n + 2)
 
     diag = b == p
-    outer = jnp.logical_or(p == 0, p == 3)
-    helper_blk = jnp.where(p == 0, 1, 2)
-    helper = both(outer, b == helper_blk)
-    giver = both(jnp.logical_not(outer), diag)
-    first = jnp.where(p == 1, 1, 0)
-    last = jnp.where(p == 2, n - 2, n - 1)
-    active = both(b >= first, b <= last)
-    go_left, go_right = both(b - 1 >= first, b > 0), both(b + 1 <= last, b < n - 1)
+    across = b == peer
+    entry = jnp.logical_or(diag, across)
+    top = pl.ds(0, half)
+    low = pl.ds(half, half)
+
+    own_top = remote(r_ref.at[top], rbuf.at[b, top], rsend.at[0], rrecv.at[b, 0], p, p)
+    own_low = remote(r_ref.at[low], stage, rsend.at[1], grecv, b, peer)
+    own_peer = remote(r_ref, rbuf.at[b], rsend.at[0], rrecv.at[b, 0], b, peer)
+    own_sib = remote(r_ref, rbuf.at[b], rsend.at[1], rrecv.at[b, 0], b, sib)
+    peer_sib = remote(rbuf.at[b], rbuf.at[b], rsend.at[2], rrecv.at[b, 0], b, sib)
+    on(jnp.logical_not(diag), own_low.start)
+    on(jnp.logical_not(diag), own_top.start)
+    on(diag, own_peer.start)
+    on(diag, own_sib.start)
+
     left, right = lax.rem(b + n - 1, n), lax.rem(b + 1, n)
-    entry_panel = 3 * lax.rem(b, 2)
-    entry = p == entry_panel
-    entry_peer = peer == entry_panel
-    staged = both(outer, b != peer)
-
-    r_stage = remote(r_ref, stage, rsend.at[0], grecv, b, peer)
-    r_more = remote(r_ref, rmore.at[b], rsend.at[0], qrecv.at[b], helper_blk, p)
-    r_end = remote(r_ref, rbuf.at[b], rsend.at[0], rrecv.at[b], p, p)
-    r_peer = remote(r_ref, rbuf.at[b], rsend.at[1], rrecv.at[b], b, peer)
-    r_sib = remote(r_ref, rbuf.at[b], rsend.at[2], rrecv.at[b], b, sib)
-    stages = both(jnp.logical_not(outer), jnp.logical_not(diag))
-    mores = both(outer, b != helper_blk)
-    on(stages, r_stage.start)
-    on(mores, r_more.start)
-    on(helper, r_end.start)
-    on(diag, r_peer.start)
-    on(diag, r_sib.start)
 
     def t_copy(src, c, way):
         return remote(src, tbuf.at[c], tsend.at[way, c], trecv.at[c], right if way else left, p)
 
-    def t_more(src, c):
-        return remote(src, tmore.at[c], msend.at[c], mrecv.at[c], b, sib)
-
-    on(go_left, t_copy(t_ref, b, 0).start)
-    on(go_right, t_copy(t_ref, b, 1).start)
+    on(b > 0, t_copy(t_ref, b, 0).start)
+    on(b < n - 1, t_copy(t_ref, b, 1).start)
     load_t.start()
     load_k.start()
     on(diag, load_r.start)
-    on(helper, load_m.start)
-    on(giver, t_more(t_ref, b).start)
-
-    r_on = remote(stage, rbuf.at[b], gsend, rrecv.at[b], peer, p)
-
-    @pl.when(staged)
-    def _():
-        r_stage.wait_recv()
-        r_on.start()
-
-    def r_move(j, way):
+
+    go_on = remote(stage, rbuf.at[b, low], gsend, rrecv.at[b, 1], peer, p)
+
+    @pl.when(jnp.logical_not(across))
+    def _():
+        own_low.wait_recv()
+        go_on.start()
+
+    mine = jnp.where(diag, 0, 1)
+
+    def r_move(j, which, way):
+        part = rbuf.at[j, pl.ds(pl.multiple_of(which * half, half), half)]
         to = peer if way == 0 else sib
-        return remote(rbuf.at[j], rbuf.at[j], rsend.at[3 + 2 * j + way], rrecv.at[j], b, to)
-
-    def r_pass(j):
-        return remote(rmore.at[j], rbuf.at[j], qsend.at[j], rrecv.at[j], p, p)
+        return remote(part, part, rsend.at[3 + j * 3 + way], rrecv.at[j, which], b, to)
 
     def arrivals(k):
         def arrive(c, way, more):
             t_copy(tbuf.at[c], c, way).wait_recv()
             on(more, t_copy(tbuf.at[c], c, way).start)
-            on(giver, t_more(tbuf.at[c], c).start)
-
-        on(both(b - k >= 0, b <= last), arrive, b - k, 1, go_right)
-        on(both(b + k < n, b >= first), arrive, b + k, 0, go_left)
-
-    def more_arrives(j):
-        remote(rmore.at[j], rmore.at[j], qsend.at[j], qrecv.at[j], b, p).wait_recv()
-        on(j != p, r_pass(j).start)
-
-    def entry_arrives(j):
-        r_move(j, 0).wait_recv()
-        r_move(j, 0).start()
-        r_move(j, 1).start()
-
-    def peer_arrives(j):
-        r_move(j, 1).wait_recv()
-        r_move(j, 1).start()
+
+        on(b - k >= 0, arrive, b - k, 1, b < n - 1)
+        on(b + k < n, arrive, b + k, 0, b > 0)
+
+    def across_arrives():
+        own_peer.wait_recv()
+        peer_sib.start()
+
+    def z_half(j):
+        r_move(j, mine, 0).wait_recv()
+        r_move(j, mine, 0).start()
+        r_move(j, mine, 1).start()
+
+    def x_half(j):
+        r_move(j, 1 - mine, 0).wait_recv()
+        r_move(j, 1 - mine, 2).start()
 
     near = [lax.rem(b + k, n) for k in (1, n - 1, 2)]
 
-    def compute(c):
-        sbuf[c] = jnp.zeros_like(sbuf[c])
-        dims = (((1,), (1,)), ((), ()))
-
-        def add(part, train, cols):
-            hi = part.astype(jnp.bfloat16)
-            lo = (part - hi.astype(jnp.float32)).astype(jnp.bfloat16)
-            for j in range(n):
-                block = train[j, :, cols]
-                sbuf[c, j] += lax.dot_general(
-                    hi, block, dims, preferred_element_type=jnp.float32
-                ) + lax.dot_general(lo, block, dims, preferred_element_type=jnp.float32)
-
+    def condition(c):
         def step(t, carry):
             cols = pl.ds(pl.multiple_of(t * tile, tile), tile)
-            add(jnp.dot(tbuf[c], kbuf[:, cols], preferred_element_type=jnp.float32), rbuf, cols)
+            part = jnp.dot(tbuf[c], kbuf[:, cols], preferred_element_type=jnp.float32)
+            hi = part.astype(jnp.bfloat16)
+            pbuf[c, :rows, cols] = hi
+            pbuf[c, rows:, cols] = (part - hi.astype(jnp.float32)).astype(jnp.bfloat16)
             return carry
 
-        def step_more(t, carry):
-            cols = pl.ds(pl.multiple_of(t * tile, tile), tile)
-            part = lax.dot_general(
-                tmore[c], kbuf[cols, :], dims, preferred_element_type=jnp.float32
+        lax.fori_loop(0, depth // tile, step, 0)
+
+    def score(c):
+        def step(j, carry):
+            both_terms = lax.dot_general(
+                pbuf[c], rbuf[j], (((1,), (1,)), ((), ())), preferred_element_type=jnp.float32
             )
-            add(part, rmore, cols)
+            sbuf[c, j] = both_terms[:rows] + both_terms[rows:]
             return carry
 
-        @pl.when(active)
-        def _():
-            lax.fori_loop(0, depth // tile, step, 0)
-
-        @pl.when(helper)
-        def _():
-            t_more(tmore.at[c], c).wait_recv()
-            lax.fori_loop(0, depth // tile, step_more, 0)
-
+        lax.fori_loop(0, n, step, 0)
         core_copy(c).start()
 
     def span(start, size):
@@ -238,41 +206,40 @@
             on(b - k >= 0, f, b - k)
             on(b + k < n, f, b + k)
 
+    on(both(entry, across), across_arrives)
+
+    @pl.when(entry)
+    def _():
+        for j in near:
+            z_half(j)
+
     arrivals(1)
 
-    @pl.when(helper)
+    @pl.when(entry)
     def _():
         for j in near:
-            more_arrives(j)
-
-    @pl.when(entry)
-    def _():
-        for j in near:
-            entry_arrives(j)
-        on(jnp.logical_not(diag), peer_arrives, b)
-
-    arrivals(2)
-
-    @pl.when(entry_peer)
-    def _():
-        on(jnp.logical_not(diag), peer_arrives, b)
-        for j in near:
-            peer_arrives(j)
-
-    @pl.when(jnp.logical_not(jnp.logical_or(entry, entry_peer)))
-    def _():
-        for j in range(n):
-            r_move(j, 1).wait_recv()
+            x_half(j)
 
     load_t.wait()
     load_k.wait()
+    condition(b)
+    at_step(1, condition)
+    arrivals(2)
+    at_step(2, condition)
+
+    @pl.when(jnp.logical_not(entry))
+    def _():
+        own_sib.wait_recv()
+        for j in near:
+            r_move(j, 0, 1).wait_recv()
+            r_move(j, 1, 1).wait_recv()
+
     on(diag, load_r.wait)
-    on(helper, load_m.wait)
-
     for k in range(n):
         if k > 2:
             arrivals(k)
-        at_step(k, compute)
+            at_step(k, condition)
+        at_step(k, score)
         at_step(k, join_cores)
         if k > 0:
             at_step(k - 1, join_chips)
@@ -297,41 +264,25 @@
             start = (q % 2) * half + (q // 2) * quarter
             out_ref[start:start + quarter, :] = home[q]
 
-    on(stages, r_stage.wait_send)
-    on(mores, r_more.wait_send)
-    on(helper, r_end.wait_send)
-    on(diag, r_peer.wait_send)
-    on(diag, r_sib.wait_send)
-    on(go_left, t_copy(t_ref, b, 0).wait_send)
-    on(go_right, t_copy(t_ref, b, 1).wait_send)
-    on(giver, t_more(t_ref, b).wait_send)
-    on(staged, r_on.wait_send)
-
-    @pl.when(helper)
+    on(jnp.logical_not(diag), own_top.wait_send)
+    on(jnp.logical_not(diag), own_low.wait_send)
+    on(diag, own_peer.wait_send)
+    on(diag, own_sib.wait_send)
+    on(b > 0, t_copy(t_ref, b, 0).wait_send)
+    on(b < n - 1, t_copy(t_ref, b, 1).wait_send)
+    on(jnp.logical_not(across), go_on.wait_send)
+    on(across, peer_sib.wait_send)
+
+    @pl.when(entry)
     def _():
         for j in near:
-            on(j != p, r_pass(j).wait_send)
-
-    @pl.when(entry)
-    def _():
-        for j in near:
-            r_move(j, 0).wait_send()
-            r_move(j, 1).wait_send()
-        on(jnp.logical_not(diag), r_move(b, 1).wait_send)
-
-    @pl.when(entry_peer)
-    def _():
-        for j in near:
-            r_move(j, 1).wait_send()
-        on(jnp.logical_not(diag), r_move(b, 1).wait_send)
-
-    def t_left_all(c, way, more):
-        on(more, t_copy(tbuf.at[c], c, way).wait_send)
-        on(giver, t_more(tbuf.at[c], c).wait_send)
+            for way in range(2):
+                r_move(j, mine, way).wait_send()
+            r_move(j, 1 - mine, 2).wait_send()
 
     for k in range(1, n):
-        on(both(b - k >= 0, b <= last), t_left_all, b - k, 1, go_right)
-        on(both(b + k < n, b >= first), t_left_all, b + k, 0, go_left)
+        on(both(b - k >= 0, b < n - 1), t_copy(tbuf.at[b - k], b - k, 1).wait_send)
+        on(both(b + k < n, b > 0), t_copy(tbuf.at[b + k], b + k, 0).wait_send)
     for c in range(n):
         core_copy(c).wait_send()
         chip_copy(c).wait_send()
@@ -352,10 +303,9 @@
         scratch_shapes=[
             pltpu.VMEM((n, rows, depth), bf16),
             pltpu.VMEM((n, rows, depth), bf16),
-            pltpu.VMEM((n, rows, depth), bf16),
-            pltpu.VMEM((n, rows, depth), bf16),
-            pltpu.VMEM((rows, depth), bf16),
+            pltpu.VMEM((rows // 2, depth), bf16),
             pltpu.VMEM((depth, depth), bf16),
+            pltpu.VMEM((n, 2 * rows, depth), bf16),
             pltpu.VMEM((n, n, rows, rows), f32),
             pltpu.VMEM((n, n, rows // 2, rows), f32),
             pltpu.VMEM((n, n, rows // 4, rows), f32),
@@ -365,12 +315,8 @@
             dma((3,)),
             dma((2, n)),
             dma((n,)),
-            dma((n,)),
-            dma((n,)),
-            dma((3 + 2 * n,)),
-            dma((n,)),
-            dma((n,)),
-            dma((n,)),
+            dma((3 + 3 * n,)),
+            dma((n, 2)),
             dma,
             dma,
             dma((n,)),

time: 188 us -> 131 us (0.70)
  Pallas kernels: 186 us -> 128 us
    pallas_call x1, Pallas kernels: 186 us -> 128 us  [fused(): pl.pallas_call(functools.partial(kernel, n, min(512, depth)), out_shape=j...]
where the time goes in v3:
time: 131 us; the launch traced here: 130 us
  Pallas kernels  128 us (98%)
  local copies, waits for them, and re-layouts  1.67 us (1%)
    pallas_call x1, Pallas kernels, fused(): pl.pallas_call(functools.partial(kernel, n, min(512, depth)), out_shape=j...  128 us

profile of v3, /device:TPU:1, one launch (start us, length us, event | category | flops | bytes accessed | tf_op | source)
XLA Modules:
  0.0 130.1 jit_solution(15123891028712621441)
XLA Ops:
  0.0 128.4 %shard_map.37 = f32[256,256]{1,0:T(8,128)} custom-call(bf16[256,2048]{1,0:T(8,128)(2,1)} %t_ref.1, bf16[256,2048]{1,0:T(8,128)(2,1)} %r_ref.1, bf16[2048,2048]{1,0:T(8,128)(2,1)} %k_ref.1), custom_call_target="tpu_custom_call" | custom-call | flops 17179869184 | bytes 10747904 | tf_op jit(solution)/shard_map/pallas_call | solution.py:298
  128.4 1.7 %copy.5 = f32[256,256]{1,0:T(8,128)} copy(f32[256,256]{1,0:T(8,128)} %shard_map.37) | data formatting | bytes 524288

commit v4 on v3

--- a/solution.py
+++ b/solution.py
@@ -41,7 +41,7 @@
 
 def kernel(
     n, tile, t_ref, r_ref, k_ref, out_ref,
-    tbuf, rbuf, stage, kbuf, pbuf, sbuf, crecv, xrecv, zrecv, fbuf, home,
+    tbuf, rbuf, stage, kbuf, pbuf, sbuf, crecv, xout, xrecv, zout, zrecv, fbuf, home,
     lsem, tsend, trecv, rsend, rrecv, gsend, grecv,
     csend, crsem, xsend, xrsem, zsend, zrsem, fsend, frsem,
 ):
@@ -180,22 +180,25 @@
         return remote(sbuf.at[c, :, sib_half], crecv.at[c], csend.at[c], crsem.at[c], b, sib)
 
     def chip_copy(c):
-        return remote(sbuf.at[c, :, peer_part], xrecv.at[c], xsend.at[c], xrsem.at[c], b, peer)
+        return remote(xout.at[c], xrecv.at[c], xsend.at[c], xrsem.at[c], b, peer)
 
     def plane_copy(c, k):
         to = lax.rem(b + k, n)
         return remote(
-            sbuf.at[c, to, own_part], zrecv.at[b, c], zsend.at[c, k - 1], zrsem.at[b, c], to, p
+            zout.at[c, to], zrecv.at[b, c], zsend.at[c, k - 1], zrsem.at[b, c], to, p
         )
 
     def join_cores(c):
         core_copy(c).wait_recv()
         sbuf[c, :, own_half] += crecv[c]
+        xout[c] = sbuf[c, :, peer_part].astype(xout.dtype)
         chip_copy(c).start()
 
     def join_chips(c):
         chip_copy(c).wait_recv()
-        sbuf[c, :, own_part] += xrecv[c]
+        total = sbuf[c, :, own_part] + xrecv[c].astype(jnp.float32)
+        sbuf[c, :, own_part] = total
+        zout[c] = total.astype(zout.dtype)
         for k in range(1, n):
             plane_copy(c, k).start()
 
@@ -206,25 +209,25 @@
             on(b - k >= 0, f, b - k)
             on(b + k < n, f, b + k)
 
-    on(both(entry, across), across_arrives)
+    on(across, across_arrives)
+    arrivals(1)
 
     @pl.when(entry)
     def _():
         for j in near:
             z_half(j)
-
-    arrivals(1)
-
-    @pl.when(entry)
-    def _():
-        for j in near:
-            x_half(j)
 
     load_t.wait()
     load_k.wait()
     condition(b)
+    arrivals(2)
+
+    @pl.when(entry)
+    def _():
+        for j in near:
+            x_half(j)
+
     at_step(1, condition)
-    arrivals(2)
     at_step(2, condition)
 
     @pl.when(jnp.logical_not(entry))
@@ -253,7 +256,7 @@
         for k in range(1, n):
             j = lax.rem(b + k, n)
             remote(zrecv.at[j, c], zrecv.at[j, c], zsend.at[c, 0], zrsem.at[j, c], j, p).wait_recv()
-            total = total + zrecv[j, c]
+            total = total + zrecv[j, c].astype(jnp.float32)
         fbuf[c] = total
         on(p != c, home_copy(c).start)
     out_ref[own_part, :] = fbuf[p]
@@ -308,8 +311,10 @@
             pltpu.VMEM((n, 2 * rows, depth), bf16),
             pltpu.VMEM((n, n, rows, rows), f32),
             pltpu.VMEM((n, n, rows // 2, rows), f32),
-            pltpu.VMEM((n, n, rows // 4, rows), f32),
-            pltpu.VMEM((n, n, rows // 4, rows), f32),
+            pltpu.VMEM((n, n, rows // 4, rows), bf16),
+            pltpu.VMEM((n, n, rows // 4, rows), bf16),
+            pltpu.VMEM((n, n, rows // 4, rows), bf16),
+            pltpu.VMEM((n, n, rows // 4, rows), bf16),
             pltpu.VMEM((n, rows // 4, rows), f32),
             pltpu.VMEM((n, rows // 4, rows), f32),
             dma((3,)),

time: 131 us -> 121 us (0.924)
  Pallas kernels: 128 us -> 119 us
    pallas_call x1, Pallas kernels: 128 us -> 119 us  [fused(): pl.pallas_call(functools.partial(kernel, n, min(512, depth)), out_shape=j...]
where the time goes in v4:
time: 121 us
  Pallas kernels  119 us (98%)
  local copies, waits for them, and re-layouts  1.67 us (1%)
    pallas_call x1, Pallas kernels, fused(): pl.pallas_call(functools.partial(kernel, n, min(512, depth)), out_shape=j...  119 us

profile of v4, /device:TPU:1, one launch (start us, length us, event | category | flops | bytes accessed | tf_op | source)
XLA Modules:
  0.0 121.1 jit_solution(17536263471370598564)
XLA Ops:
  0.0 119.4 %shard_map.37 = f32[256,256]{1,0:T(8,128)} custom-call(bf16[256,2048]{1,0:T(8,128)(2,1)} %t_ref.1, bf16[256,2048]{1,0:T(8,128)(2,1)} %r_ref.1, bf16[2048,2048]{1,0:T(8,128)(2,1)} %k_ref.1), custom_call_target="tpu_custom_call" | custom-call | flops 17179869184 | bytes 10747904 | tf_op jit(solution)/shard_map/pallas_call | solution.py:301
  119.4 1.7 %copy.5 = f32[256,256]{1,0:T(8,128)} copy(f32[256,256]{1,0:T(8,128)} %shard_map.37) | data formatting | bytes 524288

commit v5 on v4

--- a/solution.py
+++ b/solution.py
@@ -94,17 +94,22 @@
     own_sib = remote(r_ref, rbuf.at[b], rsend.at[1], rrecv.at[b, 0], b, sib)
     peer_sib = remote(rbuf.at[b], rbuf.at[b], rsend.at[2], rrecv.at[b, 0], b, sib)
     on(jnp.logical_not(diag), own_low.start)
-    on(jnp.logical_not(diag), own_top.start)
     on(diag, own_peer.start)
     on(diag, own_sib.start)
 
     left, right = lax.rem(b + n - 1, n), lax.rem(b + 1, n)
 
-    def t_copy(src, c, way):
-        return remote(src, tbuf.at[c], tsend.at[way, c], trecv.at[c], right if way else left, p)
-
-    on(b > 0, t_copy(t_ref, b, 0).start)
-    on(b < n - 1, t_copy(t_ref, b, 1).start)
+    def t_copy(src, c, way, part):
+        to = right if way else left
+        rows_of = low if part else top
+        return remote(
+            src.at[rows_of], tbuf.at[c, rows_of], tsend.at[way, c, part], trecv.at[c, part], to, p
+        )
+
+    for part in (0, 1):
+        on(b > 0, t_copy(t_ref, b, 0, part).start)
+        on(b < n - 1, t_copy(t_ref, b, 1, part).start)
+    on(jnp.logical_not(diag), own_top.start)
     load_t.start()
     load_k.start()
     on(diag, load_r.start)
@@ -125,8 +130,9 @@
 
     def arrivals(k):
         def arrive(c, way, more):
-            t_copy(tbuf.at[c], c, way).wait_recv()
-            on(more, t_copy(tbuf.at[c], c, way).start)
+            for part in (0, 1):
+                t_copy(tbuf.at[c], c, way, part).wait_recv()
+                on(more, t_copy(tbuf.at[c], c, way, part).start)
 
         on(b - k >= 0, arrive, b - k, 1, b < n - 1)
         on(b + k < n, arrive, b + k, 0, b > 0)
@@ -271,8 +277,9 @@
     on(jnp.logical_not(diag), own_low.wait_send)
     on(diag, own_peer.wait_send)
     on(diag, own_sib.wait_send)
-    on(b > 0, t_copy(t_ref, b, 0).wait_send)
-    on(b < n - 1, t_copy(t_ref, b, 1).wait_send)
+    for part in (0, 1):
+        on(b > 0, t_copy(t_ref, b, 0, part).wait_send)
+        on(b < n - 1, t_copy(t_ref, b, 1, part).wait_send)
     on(jnp.logical_not(across), go_on.wait_send)
     on(across, peer_sib.wait_send)
 
@@ -284,8 +291,9 @@
             r_move(j, 1 - mine, 2).wait_send()
 
     for k in range(1, n):
-        on(both(b - k >= 0, b < n - 1), t_copy(tbuf.at[b - k], b - k, 1).wait_send)
-        on(both(b + k < n, b > 0), t_copy(tbuf.at[b + k], b + k, 0).wait_send)
+        for part in (0, 1):
+            on(both(b - k >= 0, b < n - 1), t_copy(tbuf.at[b - k], b - k, 1, part).wait_send)
+            on(both(b + k < n, b > 0), t_copy(tbuf.at[b + k], b + k, 0, part).wait_send)
     for c in range(n):
         core_copy(c).wait_send()
         chip_copy(c).wait_send()
@@ -318,8 +326,8 @@
             pltpu.VMEM((n, rows // 4, rows), f32),
             pltpu.VMEM((n, rows // 4, rows), f32),
             dma((3,)),
-            dma((2, n)),
-            dma((n,)),
+            dma((2, n, 2)),
+            dma((n, 2)),
             dma((3 + 3 * n,)),
             dma((n, 2)),
             dma,

time: 121 us -> 115 us (0.950)
  Pallas kernels: 119 us -> 113 us
    pallas_call x1, Pallas kernels: 119 us -> 113 us  [fused(): pl.pallas_call(functools.partial(kernel, n, min(512, depth)), out_shape=j...]
where the time goes in v5:
time: 115 us
  Pallas kernels  113 us (98%)
  local copies, waits for them, and re-layouts  1.67 us (1%)
    pallas_call x1, Pallas kernels, fused(): pl.pallas_call(functools.partial(kernel, n, min(512, depth)), out_shape=j...  113 us

profile of v5, /device:TPU:1, one launch (start us, length us, event | category | flops | bytes accessed | tf_op | source)
XLA Modules:
  0.0 114.6 jit_solution(4243288062334281547)
XLA Ops:
  0.0 112.9 %shard_map.37 = f32[256,256]{1,0:T(8,128)} custom-call(bf16[256,2048]{1,0:T(8,128)(2,1)} %t_ref.1, bf16[256,2048]{1,0:T(8,128)(2,1)} %r_ref.1, bf16[2048,2048]{1,0:T(8,128)(2,1)} %k_ref.1), custom_call_target="tpu_custom_call" | custom-call | flops 17179869184 | bytes 10747904 | tf_op jit(solution)/shard_map/pallas_call | solution.py:309
  112.9 1.7 %copy.5 = f32[256,256]{1,0:T(8,128)} copy(f32[256,256]{1,0:T(8,128)} %shard_map.37) | data formatting | bytes 524288

commit v6 on v5

--- a/solution.py
+++ b/solution.py
@@ -101,12 +101,12 @@
 
     def t_copy(src, c, way, part):
         to = right if way else left
-        rows_of = low if part else top
+        rows_of = pl.ds(part * quarter, quarter)
         return remote(
             src.at[rows_of], tbuf.at[c, rows_of], tsend.at[way, c, part], trecv.at[c, part], to, p
         )
 
-    for part in (0, 1):
+    for part in range(4):
         on(b > 0, t_copy(t_ref, b, 0, part).start)
         on(b < n - 1, t_copy(t_ref, b, 1, part).start)
     on(jnp.logical_not(diag), own_top.start)
@@ -130,7 +130,7 @@
 
     def arrivals(k):
         def arrive(c, way, more):
-            for part in (0, 1):
+            for part in range(4):
                 t_copy(tbuf.at[c], c, way, part).wait_recv()
                 on(more, t_copy(tbuf.at[c], c, way, part).start)
 
@@ -277,7 +277,7 @@
     on(jnp.logical_not(diag), own_low.wait_send)
     on(diag, own_peer.wait_send)
     on(diag, own_sib.wait_send)
-    for part in (0, 1):
+    for part in range(4):
         on(b > 0, t_copy(t_ref, b, 0, part).wait_send)
         on(b < n - 1, t_copy(t_ref, b, 1, part).wait_send)
     on(jnp.logical_not(across), go_on.wait_send)
@@ -291,7 +291,7 @@
             r_move(j, 1 - mine, 2).wait_send()
 
     for k in range(1, n):
-        for part in (0, 1):
+        for part in range(4):
             on(both(b - k >= 0, b < n - 1), t_copy(tbuf.at[b - k], b - k, 1, part).wait_send)
             on(both(b + k < n, b > 0), t_copy(tbuf.at[b + k], b + k, 0, part).wait_send)
     for c in range(n):
@@ -326,8 +326,8 @@
             pltpu.VMEM((n, rows // 4, rows), f32),
             pltpu.VMEM((n, rows // 4, rows), f32),
             dma((3,)),
-            dma((2, n, 2)),
-            dma((n, 2)),
+            dma((2, n, 4)),
+            dma((n, 4)),
             dma((3 + 3 * n,)),
             dma((n, 2)),
             dma,

time: 115 us -> 116 us (level)
    pallas_call x1, Pallas kernels: 113 us -> 114 us  [fused(): pl.pallas_call(functools.partial(kernel, n, min(512, depth)), out_shape=j...]
where the time goes in v6:
time: 116 us
  Pallas kernels  114 us (98%)
  local copies, waits for them, and re-layouts  1.67 us (1%)
    pallas_call x1, Pallas kernels, fused(): pl.pallas_call(functools.partial(kernel, n, min(512, depth)), out_shape=j...  114 us

profile of v6, /device:TPU:1, one launch (start us, length us, event | category | flops | bytes accessed | tf_op | source)
XLA Modules:
  0.0 115.8 jit_solution(10991275737451684022)
XLA Ops:
  0.0 114.2 %shard_map.37 = f32[256,256]{1,0:T(8,128)} custom-call(bf16[256,2048]{1,0:T(8,128)(2,1)} %t_ref.1, bf16[256,2048]{1,0:T(8,128)(2,1)} %r_ref.1, bf16[2048,2048]{1,0:T(8,128)(2,1)} %k_ref.1), custom_call_target="tpu_custom_call" | custom-call | flops 17179869184 | bytes 10747904 | tf_op jit(solution)/shard_map/pallas_call | solution.py:309
  114.2 1.7 %copy.5 = f32[256,256]{1,0:T(8,128)} copy(f32[256,256]{1,0:T(8,128)} %shard_map.37) | data formatting | bytes 524288
